TPU v7x, 128 devices: a whole 4x4x4 slice. The times are simulated.
128 devices in a mesh: real: 4 (over y), cell: 32 (over z, x, core).
Axes of the slice: x: 4, y: 4, z: 4, core: 2. Of those that a mesh axis runs over, the one named last changes fastest.
Arguments:
- snapshots: bfloat16 [8, 2, 256, 65536], P('real', None, None, 'cell'), may hold values from -6 to 6
- quad_weights: int32 [65536], P('cell'), may hold values from 1 to 11
- triad_pairs: int32 [512, 2], replicated, may hold values from 1 to 62, as said below
- owner_counts: int32 [32], replicated, may hold values from 1 to 32, 512 in all
Outputs:
- bispectra: float32 [1024, 8, 8, 2], P('cell', 'real')
Inputs may be any that keep to these rules, and one draw needn't show every extreme that they name: `owner_counts`: the counts sum to 512, each is at least 1, and the largest is exactly 32. `triad_pairs`: for each triad k >= 1, l >= 1 and k + l <= 63.
All inputs are finite; a program needn't handle non-finite values.
Results may differ from a plain program's by a relative error of at most 0.0075.
Values may be sent and summed in bfloat16 or wider, within the bound.
No kernel may reach another device: no remote copies, remote signals or barrier semaphores. Data moves between devices by JAX's collectives and lax.ppermute only.
A program may use at most 64 MiB of HBM per device.

v0:
```python
import functools

import jax
import jax.numpy as jnp
import numpy as np
from jax import lax
from jax.experimental import pallas as pl
from jax.experimental.pallas import tpu as pltpu
from jax.sharding import PartitionSpec as P

SNAPS = 256
FREQS = 64
REALS = 8
TRIADS = 512
OWN_MOST = 32
N_REAL = 4
N_CELL = 32
XQ = 512
PARTS = ((0, 256), (256, 256))
TB = 64
WIN = 16
WIN_FIRST = 32
ROWS = 9
DFT_VMEM = 115 * 512 * 1024
VMEM_SPACE = pl.BlockSpec(memory_space=pltpu.VMEM)
SMEM_SPACE = pl.BlockSpec(memory_space=pltpu.SMEM)


def dft_table():
    times = np.arange(SNAPS)
    bins = np.arange(FREQS)
    window = 0.5 - 0.5 * np.cos(2.0 * np.pi * times / SNAPS)
    norm = np.sqrt(np.sum(window * window))
    phases = 2.0 * np.pi * ((bins[:, None] * times[None, :]) % SNAPS) / SNAPS
    table = np.concatenate([window * np.cos(phases), -window * np.sin(phases)], axis=0) / norm
    return jnp.asarray(table.astype(np.float32)).astype(jnp.bfloat16)


def dft_kernel(jobs, after, where_ref, basis_ref, snapshots_ref, *refs):
    n, refs = len(jobs), refs[after:]
    outs, bufs, basis, sems = refs[:n], refs[n : 2 * n], refs[2 * n], refs[2 * n + 1]
    table = pltpu.make_async_copy(basis_ref, basis, sems.at[n])
    table.start()
    copies = []
    for i, (s, start, width) in enumerate(jobs):
        at = pl.multiple_of(lax.rem(where_ref[0] + s, N_REAL) * XQ + start, 128)
        copies.append(
            pltpu.make_async_copy(snapshots_ref.at[:, :, :, pl.ds(at, width)], bufs[i], sems.at[i])
        )
        copies[-1].start()
    table.wait()
    for i in range(n):
        copies[i].wait()
        for r in range(2):
            for v in range(2):
                outs[i][r, v] = jnp.dot(
                    basis[...], bufs[i][r, v], preferred_element_type=jnp.float32
                ).astype(jnp.bfloat16)


def dft(where, basis, snapshots, jobs, after=()):
    n, cells = len(jobs), sum(width for _, _, width in jobs)
    return pl.pallas_call(
        functools.partial(dft_kernel, jobs, len(after)),
        in_specs=[SMEM_SPACE] + [pl.BlockSpec(memory_space=pl.ANY)] * (2 + len(after)),
        out_specs=[VMEM_SPACE] * n,
        out_shape=[jax.ShapeDtypeStruct((2, 2, 2 * FREQS, width), jnp.bfloat16) for _, _, width in jobs],
        scratch_shapes=[pltpu.VMEM((2, 2, SNAPS, width), jnp.bfloat16) for _, _, width in jobs]
        + [pltpu.VMEM((2 * FREQS, SNAPS), jnp.bfloat16), pltpu.SemaphoreType.DMA((n + 1,))],
        compiler_params=pltpu.CompilerParams(vmem_limit_bytes=DFT_VMEM),
        cost_estimate=pl.CostEstimate(
            flops=2 * 4 * 2 * FREQS * SNAPS * cells, bytes_accessed=4 * SNAPS * 2 * cells, transcendentals=0
        ),
    )(where, basis, snapshots, *after)


def triad_kernel(start, width, last, where_ref, pairs_ref, places_ref, spans_ref, p0, p1, p2, p3, w_ref, *refs):
    if last:
        before, out_ref, cf, part, left_a, left_b, full_a, full_b, acc = refs
    else:
        acc, cf, part, left_a, left_b, full_a, full_b = refs
    vx = 2 * width
    tiles = vx // 128
    me = where_ref[0]
    for s, piece in enumerate((p0, p1, p2, p3)):
        group = lax.rem(me + N_REAL - s, N_REAL)
        for r in range(2):
            for v in range(2):
                for q in range(width // 128):
                    cf[v * (width // 128) + q, pl.ds(2 * group + r, 2 * FREQS, stride=REALS), :] = piece[
                        r, v, :, q * 128 : (q + 1) * 128
                    ].astype(jnp.float32)
    weights = [
        w_ref[:, pl.ds(pl.multiple_of(me * XQ + start + q * 128, 128), 128)].astype(jnp.float32)
        for q in range(width // 128)
    ]
    weights = [jnp.broadcast_to(weight, (REALS, 128)) for weight in weights]

    def prepare(m, carry):
        re = pl.ds(pl.multiple_of(m * REALS, REALS), REALS)
        im = pl.ds(pl.multiple_of((m + FREQS) * REALS, REALS), REALS)
        rows = pl.ds(pl.multiple_of(m * 2 * REALS, 2 * REALS), 2 * REALS)
        for q in range(tiles):
            a, b = cf[q, re, :], cf[q, im, :]
            part[rows, q * 128 : (q + 1) * 128] = jnp.concatenate([a, b], axis=0).astype(jnp.bfloat16)
            part[rows, vx + q * 128 : vx + (q + 1) * 128] = jnp.concatenate([b, -a], axis=0).astype(jnp.bfloat16)
        return carry

    lax.fori_loop(0, FREQS, prepare, 0, unroll=4)
    acc[...] = jnp.zeros_like(acc)
    lane_group = lax.broadcasted_iota(jnp.int32, (REALS, 128), 1) // (2 * REALS)

    def build(left, block):
        for pair in range(TB // 2):
            rows = slice(2 * REALS * pair, 2 * REALS * (pair + 1))
            slices = []
            for h in range(2):
                word = pairs_ref[block * TB + 2 * pair + h]
                slices.append([pl.ds(pl.multiple_of(n, 2 * REALS), 2 * REALS) for n in (word & 1023, word >> 10)])
            for q in range(tiles):
                lanes = slice(q * 128, (q + 1) * 128)
                weight = weights[q % (width // 128)]
                reals, imags = [], []
                for kr, lr in slices:
                    k, l = part[kr, lanes].astype(jnp.float32), part[lr, lanes].astype(jnp.float32)
                    ak, bk, al, bl = k[:REALS], k[REALS:], l[:REALS], l[REALS:]
                    reals.append((ak * al - bk * bl) * weight)
                    imags.append((ak * bl + bk * al) * weight)
                left[rows, lanes] = jnp.concatenate(reals, axis=0).astype(jnp.bfloat16)
                left[rows, vx + q * 128 : vx + (q + 1) * 128] = jnp.concatenate(imags, axis=0).astype(jnp.bfloat16)

    def multiply(left, full, first, win=WIN):
        rows = pl.ds(pl.multiple_of(first * 2 * REALS, 2 * REALS), win * 2 * REALS)
        prod = lax.dot_general(
            left[...], part[rows, :], (((1,), (1,)), ((), ())), preferred_element_type=jnp.float32
        )
        for c in range(win // 8):
            full[c] = prod[:, c * 128 : (c + 1) * 128]

    def put(full, i, row, half, turn, want):
        tile = pltpu.roll(full[half, pl.ds(i * REALS, REALS), :], turn, 1)
        pltpu.store(acc.at[pl.ds(pl.multiple_of(row, REALS), REALS), :], tile, mask=lane_group == want)

    def extract(full, block):
        for i in range(TB):
            word = places_ref[block * TB + i]
            put(full, i, word & 1016, (word >> 10) & 3, (word >> 8) & 112, word >> 15)

    blocks = TRIADS // TB
    build(left_a, 0)
    multiply(left_a, full_a, spans_ref[0], WIN_FIRST)
    build(left_b, 1)

    def stage(left, full, block, left_next, full_last):
        multiply(left, full, spans_ref[block])
        build(left_next, jnp.minimum(block + 1, blocks - 1))
        extract(full_last, block - 1)

    def step(i, carry):
        stage(left_b, full_b, 2 * i + 1, left_a, full_a)
        stage(left_a, full_a, 2 * i + 2, left_b, full_b)
        return carry

    lax.fori_loop(0, blocks // 2 - 1, step, 0)
    stage(left_b, full_b, blocks - 1, left_a, full_a)
    extract(full_b, blocks - 1)

    def beyond(block, carry):
        high = spans_ref[blocks + block]

        def more(first):
            low = jnp.minimum(first, FREQS - WIN)
            build(left_a, block)
            multiply(left_a, full_a, low)

            def one(i, carry):
                pair, slot = pairs_ref[block * TB + i], places_ref[block * TB + i] & 1023
                at = ((pair & 1023) + (pair >> 10)) // (2 * REALS) - low
                inside = jnp.logical_and(at >= 0, at < WIN)
                at = at & (WIN - 1)
                turn = ((slot - at) & 7) * (2 * REALS)
                put(full_a, i, slot & 1016, at >> 3, turn, jnp.where(inside, slot & 7, -1))
                return carry

            lax.fori_loop(0, TB, one, 0)
            return first + WIN

        lax.while_loop(lambda first: first <= high, more, spans_ref[block] + jnp.where(block == 0, WIN_FIRST, WIN))
        return carry

    lax.fori_loop(0, blocks, beyond, 0)

    if last:
        own = w_ref[:, pl.ds(pl.multiple_of(me * XQ, 128), XQ)].astype(jnp.float32)
        square = jnp.broadcast_to(jnp.sum(own * own, axis=1, keepdims=True), (1, 128))
        for o in range(N_CELL):
            for y in range(N_REAL):
                to = ROWS * (o * N_REAL + y)
                for r in range(2):
                    rows = pl.ds(o * OWN_MOST + 2 * y + r, 4, stride=REALS)
                    out_ref[to + 4 * r : to + 4 * r + 4, :] = acc[rows, :] + before[rows, :]
                out_ref[to + 8 : to + 9, :] = square


def triads(where, plan, pieces, quad_weights, start, width, before=None):
    vx, last = 2 * width, before is not None
    sums = jax.ShapeDtypeStruct((N_CELL * OWN_MOST, 128), jnp.float32)
    sent = jax.ShapeDtypeStruct((N_CELL * N_REAL * ROWS, 128), jnp.float32)
    return pl.pallas_call(
        functools.partial(triad_kernel, start, width, last),
        in_specs=[SMEM_SPACE] * 4 + [VMEM_SPACE] * (6 if last else 5),
        out_specs=VMEM_SPACE,
        scratch_shapes=[
            pltpu.VMEM((vx // 128, 2 * FREQS * REALS, 128), jnp.float32),
            pltpu.VMEM((2 * FREQS * REALS, 2 * vx), jnp.bfloat16),
            pltpu.VMEM((TB * REALS, 2 * vx), jnp.bfloat16),
            pltpu.VMEM((TB * REALS, 2 * vx), jnp.bfloat16),
            pltpu.VMEM((WIN_FIRST // 8, TB * REALS, 128), jnp.float32),
            pltpu.VMEM((WIN_FIRST // 8, TB * REALS, 128), jnp.float32),
        ]
        + ([pltpu.VMEM(sums.shape, jnp.float32)] if last else []),
        out_shape=sent if last else sums,
        compiler_params=pltpu.CompilerParams(vmem_limit_bytes=24 * 1024 * 1024),
        cost_estimate=pl.CostEstimate(flops=20_000_000 * width, bytes_accessed=2 * 1024 * 1024, transcendentals=0),
    )(where, *plan, *pieces, quad_weights, *([before] if last else []))


def finish_kernel(received_ref, out_ref, sums):
    period = 8 * ROWS
    total = received_ref[0:period, :]
    for i in range(1, N_CELL * N_REAL * ROWS // period):
        total = total + received_ref[i * period : (i + 1) * period, :]
    sums[...] = total
    rows = [jnp.sum(sums[pl.ds(r, 8, stride=ROWS), :], axis=0, keepdims=True) for r in range(ROWS)]
    scale = 1.0 / jnp.sqrt(rows[8])
    values = jnp.concatenate([row * scale for row in rows[:8]], axis=0)
    turned = jnp.concatenate([values, jnp.zeros((120, 128), jnp.float32)], axis=0).T
    lane = lax.broadcasted_iota(jnp.int32, (2 * REALS, 128), 1)
    for i in range(2):
        placed = jnp.zeros((2 * REALS, 128), jnp.float32)
        for t in range(8):
            piece = turned[t * 2 * REALS : (t + 1) * 2 * REALS, :]
            placed = jnp.where(lane // 4 == t, pltpu.roll(piece, (4 * t - 4 * i) % 128, 1), placed)
        for c in range(2):
            for j in range(REALS):
                out_ref[i, j, c : c + 1, :] = placed[c * REALS + j : c * REALS + j + 1, :OWN_MOST]


def finish(received):
    return pl.pallas_call(
        finish_kernel,
        in_specs=[VMEM_SPACE],
        out_specs=VMEM_SPACE,
        scratch_shapes=[pltpu.VMEM((8 * ROWS, 128), jnp.float32)],
        out_shape=jax.ShapeDtypeStruct((2, REALS, 2, OWN_MOST), jnp.float32),
        compiler_params=pltpu.CompilerParams(vmem_limit_bytes=4 * 1024 * 1024),
    )(received)


def triad_plan(triad_pairs, owner_counts):
    ids = jnp.arange(TRIADS, dtype=jnp.int32)
    owners = jnp.arange(N_CELL, dtype=jnp.int32)
    ending = jnp.sum(jnp.where(owners[None, :] <= owners[:, None], owner_counts[None, :], 0), axis=1)
    past = ids[:, None] >= ending[None, :]
    owner = jnp.sum(past.astype(jnp.int32), axis=1)
    start = jnp.sum(jnp.where(past, owner_counts[None, :], 0), axis=1)
    place = ids - start
    slot = owner * OWN_MOST + (place & 3) * 8 + (place >> 2)
    first, second = triad_pairs[:, 0], triad_pairs[:, 1]
    key = (first + second) * TRIADS + ids
    rank = jnp.sum((key[None, :] < key[:, None]).astype(jnp.int32), axis=1)
    word = first + second * FREQS + slot * FREQS * FREQS
    word = jnp.sum(jnp.where(rank[None, :] == ids[:, None], word[None, :], 0), axis=1)
    first, second, slot = word & 63, (word >> 6) & 63, word >> 12
    total = (first + second).reshape(-1, TB)
    win = jnp.where(jnp.arange(TRIADS // TB) == 0, WIN_FIRST, WIN)
    low, high = jnp.minimum(total[:, 0], FREQS - win), total[:, TB - 1]
    at = (total - low[:, None]).reshape(-1)
    outside = ((total - low[:, None]) >= win[:, None]).reshape(-1).astype(jnp.int32)
    turn = (slot - at) & 7
    places = slot + (((at >> 3) & 3) << 10) + (turn << 12) + (((slot & 7) + 8 * outside) << 15)
    pairs = first * 2 * REALS + ((second * 2 * REALS) << 10)
    return pairs, places, jnp.concatenate([low, high])


def local(snapshots, quad_weights, triad_pairs, owner_counts):
    basis = dft_table()
    where = lax.axis_index("real").astype(jnp.int32).reshape(1)
    weights = quad_weights.reshape(1, -1)
    plan = triad_plan(triad_pairs, owner_counts)
    shifts = (1, 3, 2)
    (first, width), (second, width2) = PARTS
    early = tuple((s, first, width) for s in shifts) + ((0, first, width), (0, second, width2))
    early = dft(where, basis, snapshots, early)
    late = dft(where, basis, snapshots, tuple((s, second, width2) for s in shifts), (early[0],))
    away, own = [early[:3], late], early[3:]
    arrived = []
    for pieces in away:
        moved = [
            lax.ppermute(piece, "real", [(i, (i + s) % N_REAL) for i in range(N_REAL)])
            for piece, s in zip(pieces, shifts)
        ]
        arrived.append((moved[0], moved[2], moved[1]))
    sums = None
    for (start, width), pieces, here in zip(PARTS, arrived, own):
        sums = triads(where, plan, (here,) + pieces, weights, start, width, sums)
    sums = sums.reshape(N_CELL * N_REAL, 1, ROWS * 128)
    received = lax.all_to_all(sums, ("cell", "real"), split_axis=0, concat_axis=0, tiled=True)
    values = finish(received.reshape(N_CELL * N_REAL * ROWS, 128))
    return jnp.transpose(values, (3, 0, 1, 2))


def solution(mesh):
    return jax.shard_map(
        local,
        mesh=mesh,
        in_specs=(P("real", None, None, "cell"), P("cell"), P(), P()),
        out_specs=P("cell", "real", None, None),
        check_vma=False,
    )
```

profile of v0, /device:TPU:1, one launch (start us, length us, event | category | flops | bytes accessed | tf_op | source)
XLA Modules:
  0.0 66.2 jit_solution(12399270873236634044)
XLA Ops:
  0.0 0.0 copy-start.4
  0.0 0.0 copy-start.3
  0.0 0.0 copy-start.2
  0.0 3.2 %shard_map.55 = (bf16[2,2,128,256]{3,2,1,0:T(8,128)(2,1)}, bf16[2,2,128,256]{3,2,1,0:T(8,128)(2,1)}, bf16[2,2,128,256]{3,2,1,0:T(8,128)(2,1)}, bf16[2,2,128,256]{3,2,1,0:T(8,128)(2,1)}, bf16[2,2,128,256]{3,2,1,0:T(8,128)(2,1)}) custom-call(s32[1]{0:T(128)} %bitcast.where_ref, bf16[128,256]{1,0:T(8,128)(2,1)} %constant.46.basis_ref, ...), custom_call_target="tpu_custom_call" | custom-call | flops 335544320 | bytes 2621440 | tf_op jit(solution)/shard_map/pallas_call | solution.py:63
  3.2 0.0 copy-start.1
  3.2 3.8 %collective-permute-start.4 = (bf16[2,2,128,256]{3,2,1,0:T(8,128)(2,1)}, bf16[2,2,128,256]{3,2,1,0:T(8,128)(2,1)S(1)}, u32[]{:S(2)}, u32[]{:S(2)}) collective-permute-start(bf16[2,2,128,256]{3,2,1,0:T(8,128)(2,1)} %get-tuple-element.19), channel_id=1, source_target_pairs={{0,64},{32,96},{64,0},{96,32},{1,65},{33,97},{65,1},{97,33},{2,66}... | collective-permute-start | bytes 786440 | tf_op jit(solution)/shard_map/ppermute | solution.py:300
  7.1 0.8 %collective-permute-start.5 = (bf16[2,2,128,256]{3,2,1,0:T(8,128)(2,1)}, bf16[2,2,128,256]{3,2,1,0:T(8,128)(2,1)S(1)}, u32[]{:S(2)}, u32[]{:S(2)}) collective-permute-start(bf16[2,2,128,256]{3,2,1,0:T(8,128)(2,1)} %get-tuple-element.20), channel_id=1, source_target_pairs={{0,96},{32,0},{64,32},{96,64},{1,97},{33,1},{65,33},{97,65},{2,98}... | collective-permute-start | bytes 786440 | tf_op jit(solution)/shard_map/ppermute | solution.py:300
  7.8 0.7 %collective-permute-start.3 = (bf16[2,2,128,256]{3,2,1,0:T(8,128)(2,1)}, bf16[2,2,128,256]{3,2,1,0:T(8,128)(2,1)S(1)}, u32[]{:S(2)}, u32[]{:S(2)}) collective-permute-start(bf16[2,2,128,256]{3,2,1,0:T(8,128)(2,1)} %get-tuple-element.14.refs_0_), channel_id=1, source_target_pairs={{0,32},{32,64},{64,96},{96,0},{1,33},{33,65},{65,97},{97,1},{2,34}... | collective-permute-start | bytes 786440 | tf_op jit(solution)/shard_map/ppermute | solution.py:300
  8.5 2.5 %shard_map.56 = (bf16[2,2,128,256]{3,2,1,0:T(8,128)(2,1)}, bf16[2,2,128,256]{3,2,1,0:T(8,128)(2,1)}, bf16[2,2,128,256]{3,2,1,0:T(8,128)(2,1)}) custom-call(s32[1]{0:T(128)} %bitcast.where_ref, bf16[128,256]{1,0:T(8,128)(2,1)} %constant.46.basis_ref, bf16[2,2,256,2048]{3,2,1,0:T(8,128)(2,1)} %snapshots_ref.3, bf16[2,2,128,256]{3,2,1,0:T(8,128)(2,1)} %get-tuple-element.14.refs_0_), custom_call_target="tpu_custom_call" | custom-call | flops 201326592 | bytes 1572864 | tf_op jit(solution)/shard_map/pallas_call | solution.py:63
  11.1 0.5 collective-permute-start
  11.5 2.8 %collective-permute-start.1 = (bf16[2,2,128,256]{3,2,1,0:T(8,128)(2,1)}, bf16[2,2,128,256]{3,2,1,0:T(8,128)(2,1)S(1)}, u32[]{:S(2)}, u32[]{:S(2)}) collective-permute-start(bf16[2,2,128,256]{3,2,1,0:T(8,128)(2,1)} %get-tuple-element.16), channel_id=1, source_target_pairs={{0,64},{32,96},{64,0},{96,32},{1,65},{33,97},{65,1},{97,33},{2,66}... | collective-permute-start | bytes 786440 | tf_op jit(solution)/shard_map/ppermute | solution.py:300
  14.3 0.0 copy-done.4
  14.3 0.1 select_reduce_fusion.2
  14.4 0.1 convert_reduce_fusion.1
  14.5 0.0 copy-done.3
  14.6 0.2 convert_reduce_fusion
  14.8 0.2 select_reduce_fusion
  15.0 0.1 add.82
  15.1 0.2 slice_reduce_fusion.1
  15.3 0.1 pad_add_fusion.spans_ref
  15.4 0.1 ge.27
  15.5 0.1 ge.28
  15.6 0.1 sub.43
  15.6 0.1 sub.44
  15.7 0.0 collective-permute-done.4.p2
  15.7 0.3 collective-permute-start.2
  16.0 3.6 %collective-permute-done.5.p3 = bf16[2,2,128,256]{3,2,1,0:T(8,128)(2,1)S(1)} collective-permute-done((bf16[2,2,128,256]{3,2,1,0:T(8,128)(2,1)}, bf16[2,2,128,256]{3,2,1,0:T(8,128)(2,1)S(1)}, u32[]{:S(2)}, u32[]{:S(2)}) %collective-permute-start.5) | collective-permute-done | bytes 262176 | tf_op jit(solution)/shard_map/ppermute | solution.py:300
  19.6 0.0 collective-permute-done.3.p1
  19.6 0.0 copy-done.2
  19.6 0.0 copy-done.1
  19.6 0.0 copy-start
  19.7 9.3 %shard_map.57.refs_0_ = f32[1024,128]{1,0:T(8,128)S(1)} custom-call(s32[1]{0:T(128)} %bitcast.where_ref, s32[512]{0:T(512)S(1)} %get-tuple-element.32.pairs_ref, s32[512]{0:T(512)S(1)} %get-tuple-element.31.places_ref, s32[16]{0:T(128)S(1)} %pad_add_fusion.spans_ref, bf16[2,2,128,256]{3,2,1,0:T(8,128)(2,1)S(1)} %copy-done.1, ...), custom_call_target="tpu_custom_call" | custom-call | flops 5120000000 | bytes 2097152 | tf_op jit(solution)/shard_map/pallas_call | solution.py:209
  28.9 0.0 collective-permute-done.p1
  28.9 0.9 %collective-permute-done.1.p2 = bf16[2,2,128,256]{3,2,1,0:T(8,128)(2,1)S(1)} collective-permute-done((bf16[2,2,128,256]{3,2,1,0:T(8,128)(2,1)}, bf16[2,2,128,256]{3,2,1,0:T(8,128)(2,1)S(1)}, u32[]{:S(2)}, u32[]{:S(2)}) %collective-permute-start.1) | collective-permute-done | bytes 262176 | tf_op jit(solution)/shard_map/ppermute | solution.py:300
  29.9 0.5 collective-permute-done.2.p3
  30.4 0.0 copy-done
  30.4 9.5 %shard_map.58 = f32[1152,128]{1,0:T(8,128)S(1)} custom-call(s32[1]{0:T(128)} %bitcast.where_ref, s32[512]{0:T(512)S(1)} %get-tuple-element.32.pairs_ref, s32[512]{0:T(512)S(1)} %get-tuple-element.31.places_ref, s32[16]{0:T(128)S(1)} %pad_add_fusion.spans_ref, bf16[2,2,128,256]{3,2,1,0:T(8,128)(2,1)S(1)} %copy-done, ...), custom_call_target="tpu_custom_call" | custom-call | flops 5120000000 | bytes 2097152 | tf_op jit(solution)/shard_map/pallas_call | solution.py:209
  39.9 25.5 %all_to_all.5 = f32[128,1,1152]{2,1,0:T(1,128)S(1)} all-to-all(f32[128,1,1152]{2,1,0:T(1,128)S(1)} %bitcast.9), channel_id=1, replica_groups=mesh['real'=4,'cell'=32] {'cell','real'}, dimensions={0} | all-to-all | bytes 1179648 | tf_op jit(solution)/shard_map/all_to_all | solution.py:308
  65.4 0.9 %shard_map.59 = f32[2,8,2,32]{3,2,1,0:T(2,128)} custom-call(f32[1152,128]{1,0:T(8,128)S(1)} %bitcast.8), custom_call_target="tpu_custom_call" | custom-call | tf_op jit(solution)/shard_map/pallas_call | solution.py:250
  (6 shorter events, 0.1 us)
Async XLA Ops:
  0.0 14.3 %copy-start.4 = (s32[32]{0:T(128)S(1)}, s32[32]{0:T(128)}, u32[]{:S(2)}) copy-start(s32[32]{0:T(128)} %param.8) | copy-start | bytes 388
  0.0 14.5 %copy-start.3 = (s32[512,2]{0,1:T(2,128)S(1)}, s32[512,2]{0,1:T(2,128)}, u32[]{:S(2)}) copy-start(s32[512,2]{0,1:T(2,128)} %param.7) | copy-start | bytes 12292
  0.0 19.6 %copy-start.2 = (s32[2048]{0:T(1024)S(1)}, s32[2048]{0:T(1024)}, u32[]{:S(2)}) copy-start(s32[2048]{0:T(1024)} %param.6) | copy-start | bytes 24580
  3.2 16.4 %copy-start.1 = (bf16[2,2,128,256]{3,2,1,0:T(8,128)(2,1)S(1)}, bf16[2,2,128,256]{3,2,1,0:T(8,128)(2,1)}, u32[]{:S(2)}) copy-start(bf16[2,2,128,256]{3,2,1,0:T(8,128)(2,1)} %get-tuple-element.18.p0) | copy-start | bytes 786436
  3.2 12.5 %collective-permute-start.4 = (bf16[2,2,128,256]{3,2,1,0:T(8,128)(2,1)}, bf16[2,2,128,256]{3,2,1,0:T(8,128)(2,1)S(1)}, u32[]{:S(2)}, u32[]{:S(2)}) collective-permute-start(bf16[2,2,128,256]{3,2,1,0:T(8,128)(2,1)} %get-tuple-element.19), channel_id=1, source_target_pairs={{0,64},{32,96},{64,0},{96,32},{1,65},{33,97},{65,1},{97,33},{2,66}... | collective-permute-start | bytes 786440 | tf_op jit(solution)/shard_map/ppermute | solution.py:300
  7.1 12.6 %collective-permute-start.5 = (bf16[2,2,128,256]{3,2,1,0:T(8,128)(2,1)}, bf16[2,2,128,256]{3,2,1,0:T(8,128)(2,1)S(1)}, u32[]{:S(2)}, u32[]{:S(2)}) collective-permute-start(bf16[2,2,128,256]{3,2,1,0:T(8,128)(2,1)} %get-tuple-element.20), channel_id=1, source_target_pairs={{0,96},{32,0},{64,32},{96,64},{1,97},{33,1},{65,33},{97,65},{2,98}... | collective-permute-start | bytes 786440 | tf_op jit(solution)/shard_map/ppermute | solution.py:300
  7.8 11.8 %collective-permute-start.3 = (bf16[2,2,128,256]{3,2,1,0:T(8,128)(2,1)}, bf16[2,2,128,256]{3,2,1,0:T(8,128)(2,1)S(1)}, u32[]{:S(2)}, u32[]{:S(2)}) collective-permute-start(bf16[2,2,128,256]{3,2,1,0:T(8,128)(2,1)} %get-tuple-element.14.refs_0_), channel_id=1, source_target_pairs={{0,32},{32,64},{64,96},{96,0},{1,33},{33,65},{65,97},{97,1},{2,34}... | collective-permute-start | bytes 786440 | tf_op jit(solution)/shard_map/ppermute | solution.py:300
  11.1 17.9 %collective-permute-start = (bf16[2,2,128,256]{3,2,1,0:T(8,128)(2,1)}, bf16[2,2,128,256]{3,2,1,0:T(8,128)(2,1)S(1)}, u32[]{:S(2)}, u32[]{:S(2)}) collective-permute-start(bf16[2,2,128,256]{3,2,1,0:T(8,128)(2,1)} %get-tuple-element.15), channel_id=1, source_target_pairs={{0,32},{32,64},{64,96},{96,0},{1,33},{33,65},{65,97},{97,1},{2,34}... | collective-permute-start | bytes 786440 | tf_op jit(solution)/shard_map/ppermute | solution.py:300
  11.5 18.3 %collective-permute-start.1 = (bf16[2,2,128,256]{3,2,1,0:T(8,128)(2,1)}, bf16[2,2,128,256]{3,2,1,0:T(8,128)(2,1)S(1)}, u32[]{:S(2)}, u32[]{:S(2)}) collective-permute-start(bf16[2,2,128,256]{3,2,1,0:T(8,128)(2,1)} %get-tuple-element.16), channel_id=1, source_target_pairs={{0,64},{32,96},{64,0},{96,32},{1,65},{33,97},{65,1},{97,33},{2,66}... | collective-permute-start | bytes 786440 | tf_op jit(solution)/shard_map/ppermute | solution.py:300
  15.7 14.6 %collective-permute-start.2 = (bf16[2,2,128,256]{3,2,1,0:T(8,128)(2,1)}, bf16[2,2,128,256]{3,2,1,0:T(8,128)(2,1)S(1)}, u32[]{:S(2)}, u32[]{:S(2)}) collective-permute-start(bf16[2,2,128,256]{3,2,1,0:T(8,128)(2,1)} %get-tuple-element.17), channel_id=1, source_target_pairs={{0,96},{32,0},{64,32},{96,64},{1,97},{33,1},{65,33},{97,65},{2,98}... | collective-permute-start | bytes 786440 | tf_op jit(solution)/shard_map/ppermute | solution.py:300
  19.6 10.7 %copy-start = (bf16[2,2,128,256]{3,2,1,0:T(8,128)(2,1)S(1)}, bf16[2,2,128,256]{3,2,1,0:T(8,128)(2,1)}, u32[]{:S(2)}) copy-start(bf16[2,2,128,256]{3,2,1,0:T(8,128)(2,1)} %get-tuple-element.13.p0) | copy-start | bytes 786436
where the time goes:
time: 66.4 us; the launch traced here: 66.2 us
  blocking collectives  25.5 us (38%)
  Pallas kernels  25.4 us (38%)
  starting transfers between devices  8.78 us (13%)
  waiting for transfers between devices  5.07 us (8%)
  other arithmetic  1 us (2%)
    all_to_all x1, blocking collectives, local(): lax.all_to_all(sums, ('cell', 'real'), split_axis=0, concat_axis=0, tiled...  25.5 us
    pallas_call x2, Pallas kernels, triads(): pl.pallas_call(functools.partial(triad_kernel, start, width, last), in_sp...  18.8 us
    ppermute x6, starting transfers between devices, local(): lax.ppermute(piece, 'real', [(i, (i + s) % N_REAL) for i in range(N_REAL)])  8.78 us
    pallas_call x2, Pallas kernels, dft(): pl.pallas_call(functools.partial(dft_kernel, jobs, len(after)), in_specs=...  5.75 us
    ppermute x6, waiting for transfers between devices, local(): lax.ppermute(piece, 'real', [(i, (i + s) % N_REAL) for i in range(N_REAL)])  5.07 us
  transfers between devices with their start and end apart: 6, of which 3 were waited for; matrix products, arithmetic and copies ran while one was open for 2% of the time, Pallas kernels for 18%

commit v1 on v0

--- a/solution.py
+++ b/solution.py
@@ -188,7 +188,10 @@
         lax.while_loop(lambda first: first <= high, more, spans_ref[block] + jnp.where(block == 0, WIN_FIRST, WIN))
         return carry
 
-    lax.fori_loop(0, blocks, beyond, 0)
+    @pl.when(spans_ref[2 * blocks] > 0)
+    def _():
+        lax.fori_loop(0, blocks, beyond, 0)
+
 
     if last:
         own = w_ref[:, pl.ds(pl.multiple_of(me * XQ, 128), XQ)].astype(jnp.float32)
@@ -280,14 +283,13 @@
     turn = (slot - at) & 7
     places = slot + (((at >> 3) & 3) << 10) + (turn << 12) + (((slot & 7) + 8 * outside) << 15)
     pairs = first * 2 * REALS + ((second * 2 * REALS) << 10)
-    return pairs, places, jnp.concatenate([low, high])
+    return pairs, places, jnp.concatenate([low, high, jnp.max(outside, keepdims=True)])
 
 
 def local(snapshots, quad_weights, triad_pairs, owner_counts):
     basis = dft_table()
     where = lax.axis_index("real").astype(jnp.int32).reshape(1)
     weights = quad_weights.reshape(1, -1)
-    plan = triad_plan(triad_pairs, owner_counts)
     shifts = (1, 3, 2)
     (first, width), (second, width2) = PARTS
     early = tuple((s, first, width) for s in shifts) + ((0, first, width), (0, second, width2))
@@ -301,6 +303,9 @@
             for piece, s in zip(pieces, shifts)
         ]
         arrived.append((moved[0], moved[2], moved[1]))
+    later_pairs, ready = lax.optimization_barrier((triad_pairs, arrived[0][1]))
+    arrived[0] = (arrived[0][0], ready, arrived[0][2])
+    plan = triad_plan(later_pairs, owner_counts)
     sums = None
     for (start, width), pieces, here in zip(PARTS, arrived, own):
         sums = triads(where, plan, (here,) + pieces, weights, start, width, sums)

time: 66.4 us -> 66.3 us (level)
  waiting for transfers between devices: 5.07 us -> 2.97 us
  other arithmetic: 1 us -> 2.21 us
  starting transfers between devices: 8.78 us -> 9.66 us
    ppermute x6, waiting for transfers between devices: 5.07 us -> 2.97 us  [local(): lax.ppermute(piece, 'real', [(i, (i + s) % N_REAL) for i in range(N_REAL)])]
    ppermute x6, starting transfers between devices: 8.78 us -> 9.66 us  [local(): lax.ppermute(piece, 'real', [(i, (i + s) % N_REAL) for i in range(N_REAL)])]
  transfers between devices with their start and end apart: 6 -> 6, of which waited for: 3 -> 3; matrix products, arithmetic and copies ran while one was open for 2% -> 4% of each run, Pallas kernels for 18% -> 18%
where the time goes in v1:
time: 66.3 us; the launch traced here: 66.1 us
  blocking collectives  25.5 us (38%)
  Pallas kernels  25.3 us (38%)
  starting transfers between devices  9.66 us (15%)
  waiting for transfers between devices  2.97 us (4%)
  other arithmetic  2.21 us (3%)
    all_to_all x1, blocking collectives, local(): lax.all_to_all(sums, ('cell', 'real'), split_axis=0, concat_axis=0, tiled...  25.5 us
    pallas_call x2, Pallas kernels, triads(): pl.pallas_call(functools.partial(triad_kernel, start, width, last), in_sp...  18.7 us
    ppermute x6, starting transfers between devices, local(): lax.ppermute(piece, 'real', [(i, (i + s) % N_REAL) for i in range(N_REAL)])  9.66 us
    pallas_call x2, Pallas kernels, dft(): pl.pallas_call(functools.partial(dft_kernel, jobs, len(after)), in_specs=...  5.75 us
    ppermute x6, waiting for transfers between devices, local(): lax.ppermute(piece, 'real', [(i, (i + s) % N_REAL) for i in range(N_REAL)])  2.97 us
  transfers between devices with their start and end apart: 6, of which 3 were waited for; matrix products, arithmetic and copies ran while one was open for 4% of the time, Pallas kernels for 18%

profile of v1, /device:TPU:1, one launch (start us, length us, event | category | flops | bytes accessed | tf_op | source)
XLA Modules:
  0.0 66.1 jit_solution(4886806061738973112)
XLA Ops:
  0.0 0.0 copy-start.4
  0.0 0.0 copy-start.3
  0.0 0.0 copy-start.2
  0.0 3.2 %shard_map.55 = (bf16[2,2,128,256]{3,2,1,0:T(8,128)(2,1)}, bf16[2,2,128,256]{3,2,1,0:T(8,128)(2,1)}, bf16[2,2,128,256]{3,2,1,0:T(8,128)(2,1)}, bf16[2,2,128,256]{3,2,1,0:T(8,128)(2,1)}, bf16[2,2,128,256]{3,2,1,0:T(8,128)(2,1)}) custom-call(s32[1]{0:T(128)} %bitcast.where_ref, bf16[128,256]{1,0:T(8,128)(2,1)} %constant.48.basis_ref, ...), custom_call_target="tpu_custom_call" | custom-call | flops 335544320 | bytes 2621440 | tf_op jit(solution)/shard_map/pallas_call | solution.py:63
  3.2 0.0 copy-start.1
  3.2 3.8 %collective-permute-start = (bf16[2,2,128,256]{3,2,1,0:T(8,128)(2,1)}, bf16[2,2,128,256]{3,2,1,0:T(8,128)(2,1)S(1)}, u32[]{:S(2)}, u32[]{:S(2)}) collective-permute-start(bf16[2,2,128,256]{3,2,1,0:T(8,128)(2,1)} %get-tuple-element.15), channel_id=1, source_target_pairs={{0,64},{32,96},{64,0},{96,32},{1,65},{33,97},{65,1},{97,33},{2,66}... | collective-permute-start | bytes 786440 | tf_op jit(solution)/shard_map/ppermute | solution.py:302
  7.1 0.8 %collective-permute-start.5 = (bf16[2,2,128,256]{3,2,1,0:T(8,128)(2,1)}, bf16[2,2,128,256]{3,2,1,0:T(8,128)(2,1)S(1)}, u32[]{:S(2)}, u32[]{:S(2)}) collective-permute-start(bf16[2,2,128,256]{3,2,1,0:T(8,128)(2,1)} %get-tuple-element.24), channel_id=1, source_target_pairs={{0,96},{32,0},{64,32},{96,64},{1,97},{33,1},{65,33},{97,65},{2,98}... | collective-permute-start | bytes 786440 | tf_op jit(solution)/shard_map/ppermute | solution.py:302
  7.8 0.7 %collective-permute-start.4 = (bf16[2,2,128,256]{3,2,1,0:T(8,128)(2,1)}, bf16[2,2,128,256]{3,2,1,0:T(8,128)(2,1)S(1)}, u32[]{:S(2)}, u32[]{:S(2)}) collective-permute-start(bf16[2,2,128,256]{3,2,1,0:T(8,128)(2,1)} %get-tuple-element.18.refs_0_), channel_id=1, source_target_pairs={{0,32},{32,64},{64,96},{96,0},{1,33},{33,65},{65,97},{97,1},{2,34}... | collective-permute-start | bytes 786440 | tf_op jit(solution)/shard_map/ppermute | solution.py:302
  8.5 2.5 %shard_map.56 = (bf16[2,2,128,256]{3,2,1,0:T(8,128)(2,1)}, bf16[2,2,128,256]{3,2,1,0:T(8,128)(2,1)}, bf16[2,2,128,256]{3,2,1,0:T(8,128)(2,1)}) custom-call(s32[1]{0:T(128)} %bitcast.where_ref, bf16[128,256]{1,0:T(8,128)(2,1)} %constant.48.basis_ref, bf16[2,2,256,2048]{3,2,1,0:T(8,128)(2,1)} %snapshots_ref.3, bf16[2,2,128,256]{3,2,1,0:T(8,128)(2,1)} %get-tuple-element.18.refs_0_), custom_call_target="tpu_custom_call" | custom-call | flops 201326592 | bytes 1572864 | tf_op jit(solution)/shard_map/pallas_call | solution.py:63
  11.1 0.5 collective-permute-start.1
  11.5 2.8 %collective-permute-start.2 = (bf16[2,2,128,256]{3,2,1,0:T(8,128)(2,1)}, bf16[2,2,128,256]{3,2,1,0:T(8,128)(2,1)S(1)}, u32[]{:S(2)}, u32[]{:S(2)}) collective-permute-start(bf16[2,2,128,256]{3,2,1,0:T(8,128)(2,1)} %get-tuple-element.20), channel_id=1, source_target_pairs={{0,64},{32,96},{64,0},{96,32},{1,65},{33,97},{65,1},{97,33},{2,66}... | collective-permute-start | bytes 786440 | tf_op jit(solution)/shard_map/ppermute | solution.py:302
  14.3 0.1 ge.31
  14.4 0.1 ge.32
  14.5 0.0 copy-done.4
  14.5 0.1 select_reduce_fusion.2
  14.6 0.1 convert_reduce_fusion.1
  14.7 0.0 collective-permute-done.p2
  14.7 1.1 %collective-permute-start.3 = (bf16[2,2,128,256]{3,2,1,0:T(8,128)(2,1)}, bf16[2,2,128,256]{3,2,1,0:T(8,128)(2,1)S(1)}, u32[]{:S(2)}, u32[]{:S(2)}) collective-permute-start(bf16[2,2,128,256]{3,2,1,0:T(8,128)(2,1)} %get-tuple-element.21), channel_id=1, source_target_pairs={{0,96},{32,0},{64,32},{96,64},{1,97},{33,1},{65,33},{97,65},{2,98}... | collective-permute-start | bytes 786440 | tf_op jit(solution)/shard_map/ppermute | solution.py:302
  15.8 0.0 copy-done.3
  15.9 0.2 convert_reduce_fusion
  16.1 0.2 select_reduce_fusion
  16.3 0.1 add.86
  16.4 0.2 slice_reduce_fusion.1
  16.6 0.1 sub.47
  16.7 0.1 sub.48
  16.8 0.6 convert_reduce_fusion.2
  17.4 0.6 pad_add_fusion.spans_ref
  18.1 1.6 %collective-permute-done.5.p3 = bf16[2,2,128,256]{3,2,1,0:T(8,128)(2,1)S(1)} collective-permute-done((bf16[2,2,128,256]{3,2,1,0:T(8,128)(2,1)}, bf16[2,2,128,256]{3,2,1,0:T(8,128)(2,1)S(1)}, u32[]{:S(2)}, u32[]{:S(2)}) %collective-permute-start.5) | collective-permute-done | bytes 262176 | tf_op jit(solution)/shard_map/ppermute | solution.py:302
  19.7 0.0 collective-permute-done.4.p1
  19.7 0.0 copy-done.2
  19.7 0.0 copy-done.1
  19.7 0.0 copy-start
  19.7 9.3 %shard_map.57.refs_0_ = f32[1024,128]{1,0:T(8,128)S(1)} custom-call(s32[1]{0:T(128)} %bitcast.where_ref, s32[512]{0:T(512)S(1)} %get-tuple-element.38.pairs_ref, s32[512]{0:T(512)S(1)} %get-tuple-element.37.places_ref, s32[17]{0:T(128)S(1)} %pad_add_fusion.spans_ref, bf16[2,2,128,256]{3,2,1,0:T(8,128)(2,1)S(1)} %copy-done.1, ...), custom_call_target="tpu_custom_call" | custom-call | flops 5120000000 | bytes 2097152 | tf_op jit(solution)/shard_map/pallas_call | solution.py:212
  29.0 0.0 collective-permute-done.1.p1
  29.0 0.9 %collective-permute-done.2.p2 = bf16[2,2,128,256]{3,2,1,0:T(8,128)(2,1)S(1)} collective-permute-done((bf16[2,2,128,256]{3,2,1,0:T(8,128)(2,1)}, bf16[2,2,128,256]{3,2,1,0:T(8,128)(2,1)S(1)}, u32[]{:S(2)}, u32[]{:S(2)}) %collective-permute-start.2) | collective-permute-done | bytes 262176 | tf_op jit(solution)/shard_map/ppermute | solution.py:302
  29.9 0.5 collective-permute-done.3.p3
  30.4 0.0 copy-done
  30.4 9.4 %shard_map.58 = f32[1152,128]{1,0:T(8,128)S(1)} custom-call(s32[1]{0:T(128)} %bitcast.where_ref, s32[512]{0:T(512)S(1)} %get-tuple-element.38.pairs_ref, s32[512]{0:T(512)S(1)} %get-tuple-element.37.places_ref, s32[17]{0:T(128)S(1)} %pad_add_fusion.spans_ref, bf16[2,2,128,256]{3,2,1,0:T(8,128)(2,1)S(1)} %copy-done, ...), custom_call_target="tpu_custom_call" | custom-call | flops 5120000000 | bytes 2097152 | tf_op jit(solution)/shard_map/pallas_call | solution.py:212
  39.8 25.5 %all_to_all.5 = f32[128,1,1152]{2,1,0:T(1,128)S(1)} all-to-all(f32[128,1,1152]{2,1,0:T(1,128)S(1)} %bitcast.10), channel_id=1, replica_groups=mesh['real'=4,'cell'=32] {'cell','real'}, dimensions={0} | all-to-all | bytes 1179648 | tf_op jit(solution)/shard_map/all_to_all | solution.py:313
  65.3 0.9 %shard_map.59 = f32[2,8,2,32]{3,2,1,0:T(2,128)} custom-call(f32[1152,128]{1,0:T(8,128)S(1)} %bitcast.9), custom_call_target="tpu_custom_call" | custom-call | tf_op jit(solution)/shard_map/pallas_call | solution.py:253
  (6 shorter events, 0.0 us)
Async XLA Ops:
  0.0 14.5 %copy-start.4 = (s32[32]{0:T(128)S(1)}, s32[32]{0:T(128)}, u32[]{:S(2)}) copy-start(s32[32]{0:T(128)} %param.8) | copy-start | bytes 388
  0.0 15.8 %copy-start.3 = (s32[512,2]{0,1:T(2,128)S(1)}, s32[512,2]{0,1:T(2,128)}, u32[]{:S(2)}) copy-start(s32[512,2]{0,1:T(2,128)} %param.7) | copy-start | bytes 12292
  0.0 19.7 %copy-start.2 = (s32[2048]{0:T(1024)S(1)}, s32[2048]{0:T(1024)}, u32[]{:S(2)}) copy-start(s32[2048]{0:T(1024)} %param.6) | copy-start | bytes 24580
  3.2 16.4 %copy-start.1 = (bf16[2,2,128,256]{3,2,1,0:T(8,128)(2,1)S(1)}, bf16[2,2,128,256]{3,2,1,0:T(8,128)(2,1)}, u32[]{:S(2)}) copy-start(bf16[2,2,128,256]{3,2,1,0:T(8,128)(2,1)} %get-tuple-element.22.p0) | copy-start | bytes 786436
  3.2 11.4 %collective-permute-start = (bf16[2,2,128,256]{3,2,1,0:T(8,128)(2,1)}, bf16[2,2,128,256]{3,2,1,0:T(8,128)(2,1)S(1)}, u32[]{:S(2)}, u32[]{:S(2)}) collective-permute-start(bf16[2,2,128,256]{3,2,1,0:T(8,128)(2,1)} %get-tuple-element.15), channel_id=1, source_target_pairs={{0,64},{32,96},{64,0},{96,32},{1,65},{33,97},{65,1},{97,33},{2,66}... | collective-permute-start | bytes 786440 | tf_op jit(solution)/shard_map/ppermute | solution.py:302
  7.1 12.6 %collective-permute-start.5 = (bf16[2,2,128,256]{3,2,1,0:T(8,128)(2,1)}, bf16[2,2,128,256]{3,2,1,0:T(8,128)(2,1)S(1)}, u32[]{:S(2)}, u32[]{:S(2)}) collective-permute-start(bf16[2,2,128,256]{3,2,1,0:T(8,128)(2,1)} %get-tuple-element.24), channel_id=1, source_target_pairs={{0,96},{32,0},{64,32},{96,64},{1,97},{33,1},{65,33},{97,65},{2,98}... | collective-permute-start | bytes 786440 | tf_op jit(solution)/shard_map/ppermute | solution.py:302
  7.8 11.8 %collective-permute-start.4 = (bf16[2,2,128,256]{3,2,1,0:T(8,128)(2,1)}, bf16[2,2,128,256]{3,2,1,0:T(8,128)(2,1)S(1)}, u32[]{:S(2)}, u32[]{:S(2)}) collective-permute-start(bf16[2,2,128,256]{3,2,1,0:T(8,128)(2,1)} %get-tuple-element.18.refs_0_), channel_id=1, source_target_pairs={{0,32},{32,64},{64,96},{96,0},{1,33},{33,65},{65,97},{97,1},{2,34}... | collective-permute-start | bytes 786440 | tf_op jit(solution)/shard_map/ppermute | solution.py:302
  11.1 17.9 %collective-permute-start.1 = (bf16[2,2,128,256]{3,2,1,0:T(8,128)(2,1)}, bf16[2,2,128,256]{3,2,1,0:T(8,128)(2,1)S(1)}, u32[]{:S(2)}, u32[]{:S(2)}) collective-permute-start(bf16[2,2,128,256]{3,2,1,0:T(8,128)(2,1)} %get-tuple-element.19), channel_id=1, source_target_pairs={{0,32},{32,64},{64,96},{96,0},{1,33},{33,65},{65,97},{97,1},{2,34}... | collective-permute-start | bytes 786440 | tf_op jit(solution)/shard_map/ppermute | solution.py:302
  11.5 18.3 %collective-permute-start.2 = (bf16[2,2,128,256]{3,2,1,0:T(8,128)(2,1)}, bf16[2,2,128,256]{3,2,1,0:T(8,128)(2,1)S(1)}, u32[]{:S(2)}, u32[]{:S(2)}) collective-permute-start(bf16[2,2,128,256]{3,2,1,0:T(8,128)(2,1)} %get-tuple-element.20), channel_id=1, source_target_pairs={{0,64},{32,96},{64,0},{96,32},{1,65},{33,97},{65,1},{97,33},{2,66}... | collective-permute-start | bytes 786440 | tf_op jit(solution)/shard_map/ppermute | solution.py:302
  14.7 15.7 %collective-permute-start.3 = (bf16[2,2,128,256]{3,2,1,0:T(8,128)(2,1)}, bf16[2,2,128,256]{3,2,1,0:T(8,128)(2,1)S(1)}, u32[]{:S(2)}, u32[]{:S(2)}) collective-permute-start(bf16[2,2,128,256]{3,2,1,0:T(8,128)(2,1)} %get-tuple-element.21), channel_id=1, source_target_pairs={{0,96},{32,0},{64,32},{96,64},{1,97},{33,1},{65,33},{97,65},{2,98}... | collective-permute-start | bytes 786440 | tf_op jit(solution)/shard_map/ppermute | solution.py:302
  19.7 10.7 %copy-start = (bf16[2,2,128,256]{3,2,1,0:T(8,128)(2,1)S(1)}, bf16[2,2,128,256]{3,2,1,0:T(8,128)(2,1)}, u32[]{:S(2)}) copy-start(bf16[2,2,128,256]{3,2,1,0:T(8,128)(2,1)} %get-tuple-element.17.p0) | copy-start | bytes 786436

commit v2 on v0

--- a/solution.py
+++ b/solution.py
@@ -195,7 +195,7 @@
         square = jnp.broadcast_to(jnp.sum(own * own, axis=1, keepdims=True), (1, 128))
         for o in range(N_CELL):
             for y in range(N_REAL):
-                to = ROWS * (o * N_REAL + y)
+                to = ROWS * (y * N_CELL + o)
                 for r in range(2):
                     rows = pl.ds(o * OWN_MOST + 2 * y + r, 4, stride=REALS)
                     out_ref[to + 4 * r : to + 4 * r + 4, :] = acc[rows, :] + before[rows, :]
@@ -305,7 +305,7 @@
     for (start, width), pieces, here in zip(PARTS, arrived, own):
         sums = triads(where, plan, (here,) + pieces, weights, start, width, sums)
     sums = sums.reshape(N_CELL * N_REAL, 1, ROWS * 128)
-    received = lax.all_to_all(sums, ("cell", "real"), split_axis=0, concat_axis=0, tiled=True)
+    received = lax.all_to_all(sums, ("real", "cell"), split_axis=0, concat_axis=0, tiled=True)
     values = finish(received.reshape(N_CELL * N_REAL * ROWS, 128))
     return jnp.transpose(values, (3, 0, 1, 2))
 

time: 66.4 us -> 66.2 us (level)
  no operation moved by 1% of the time
where the time goes in v2:
time: 66.2 us; the launch traced here: 66.1 us
  Pallas kernels  25.4 us (38%)
  blocking collectives  25.3 us (38%)
  starting transfers between devices  8.78 us (13%)
  waiting for transfers between devices  5.07 us (8%)
  other arithmetic  1 us (2%)
    all_to_all x1, blocking collectives, local(): lax.all_to_all(sums, ('real', 'cell'), split_axis=0, concat_axis=0, tiled...  25.3 us
    pallas_call x2, Pallas kernels, triads(): pl.pallas_call(functools.partial(triad_kernel, start, width, last), in_sp...  18.8 us
    ppermute x6, starting transfers between devices, local(): lax.ppermute(piece, 'real', [(i, (i + s) % N_REAL) for i in range(N_REAL)])  8.78 us
    pallas_call x2, Pallas kernels, dft(): pl.pallas_call(functools.partial(dft_kernel, jobs, len(after)), in_specs=...  5.75 us
    ppermute x6, waiting for transfers between devices, local(): lax.ppermute(piece, 'real', [(i, (i + s) % N_REAL) for i in range(N_REAL)])  5.07 us
  transfers between devices with their start and end apart: 6, of which 3 were waited for; matrix products, arithmetic and copies ran while one was open for 2% of the time, Pallas kernels for 18%

profile of v2, /device:TPU:1, one launch (start us, length us, event | category | flops | bytes accessed | tf_op | source)
XLA Modules:
  0.0 66.1 jit_solution(897401123615465240)
XLA Ops:
  0.0 0.0 copy-start.4
  0.0 0.0 copy-start.3
  0.0 0.0 copy-start.2
  0.0 3.2 %shard_map.55 = (bf16[2,2,128,256]{3,2,1,0:T(8,128)(2,1)}, bf16[2,2,128,256]{3,2,1,0:T(8,128)(2,1)}, bf16[2,2,128,256]{3,2,1,0:T(8,128)(2,1)}, bf16[2,2,128,256]{3,2,1,0:T(8,128)(2,1)}, bf16[2,2,128,256]{3,2,1,0:T(8,128)(2,1)}) custom-call(s32[1]{0:T(128)} %bitcast.where_ref, bf16[128,256]{1,0:T(8,128)(2,1)} %constant.46.basis_ref, ...), custom_call_target="tpu_custom_call" | custom-call | flops 335544320 | bytes 2621440 | tf_op jit(solution)/shard_map/pallas_call | solution.py:63
  3.2 0.0 copy-start.1
  3.2 3.8 %collective-permute-start.4 = (bf16[2,2,128,256]{3,2,1,0:T(8,128)(2,1)}, bf16[2,2,128,256]{3,2,1,0:T(8,128)(2,1)S(1)}, u32[]{:S(2)}, u32[]{:S(2)}) collective-permute-start(bf16[2,2,128,256]{3,2,1,0:T(8,128)(2,1)} %get-tuple-element.19), channel_id=1, source_target_pairs={{0,64},{32,96},{64,0},{96,32},{1,65},{33,97},{65,1},{97,33},{2,66}... | collective-permute-start | bytes 786440 | tf_op jit(solution)/shard_map/ppermute | solution.py:300
  7.1 0.8 %collective-permute-start.5 = (bf16[2,2,128,256]{3,2,1,0:T(8,128)(2,1)}, bf16[2,2,128,256]{3,2,1,0:T(8,128)(2,1)S(1)}, u32[]{:S(2)}, u32[]{:S(2)}) collective-permute-start(bf16[2,2,128,256]{3,2,1,0:T(8,128)(2,1)} %get-tuple-element.20), channel_id=1, source_target_pairs={{0,96},{32,0},{64,32},{96,64},{1,97},{33,1},{65,33},{97,65},{2,98}... | collective-permute-start | bytes 786440 | tf_op jit(solution)/shard_map/ppermute | solution.py:300
  7.8 0.7 %collective-permute-start.3 = (bf16[2,2,128,256]{3,2,1,0:T(8,128)(2,1)}, bf16[2,2,128,256]{3,2,1,0:T(8,128)(2,1)S(1)}, u32[]{:S(2)}, u32[]{:S(2)}) collective-permute-start(bf16[2,2,128,256]{3,2,1,0:T(8,128)(2,1)} %get-tuple-element.14.refs_0_), channel_id=1, source_target_pairs={{0,32},{32,64},{64,96},{96,0},{1,33},{33,65},{65,97},{97,1},{2,34}... | collective-permute-start | bytes 786440 | tf_op jit(solution)/shard_map/ppermute | solution.py:300
  8.5 2.5 %shard_map.56 = (bf16[2,2,128,256]{3,2,1,0:T(8,128)(2,1)}, bf16[2,2,128,256]{3,2,1,0:T(8,128)(2,1)}, bf16[2,2,128,256]{3,2,1,0:T(8,128)(2,1)}) custom-call(s32[1]{0:T(128)} %bitcast.where_ref, bf16[128,256]{1,0:T(8,128)(2,1)} %constant.46.basis_ref, bf16[2,2,256,2048]{3,2,1,0:T(8,128)(2,1)} %snapshots_ref.3, bf16[2,2,128,256]{3,2,1,0:T(8,128)(2,1)} %get-tuple-element.14.refs_0_), custom_call_target="tpu_custom_call" | custom-call | flops 201326592 | bytes 1572864 | tf_op jit(solution)/shard_map/pallas_call | solution.py:63
  11.1 0.5 collective-permute-start
  11.5 2.8 %collective-permute-start.1 = (bf16[2,2,128,256]{3,2,1,0:T(8,128)(2,1)}, bf16[2,2,128,256]{3,2,1,0:T(8,128)(2,1)S(1)}, u32[]{:S(2)}, u32[]{:S(2)}) collective-permute-start(bf16[2,2,128,256]{3,2,1,0:T(8,128)(2,1)} %get-tuple-element.16), channel_id=1, source_target_pairs={{0,64},{32,96},{64,0},{96,32},{1,65},{33,97},{65,1},{97,33},{2,66}... | collective-permute-start | bytes 786440 | tf_op jit(solution)/shard_map/ppermute | solution.py:300
  14.3 0.0 copy-done.4
  14.3 0.1 select_reduce_fusion.2
  14.4 0.1 convert_reduce_fusion.1
  14.5 0.0 copy-done.3
  14.6 0.2 convert_reduce_fusion
  14.8 0.2 select_reduce_fusion
  15.0 0.1 add.82
  15.1 0.2 slice_reduce_fusion.1
  15.3 0.1 pad_add_fusion.spans_ref
  15.4 0.1 ge.27
  15.5 0.1 ge.28
  15.6 0.1 sub.43
  15.6 0.1 sub.44
  15.7 0.0 collective-permute-done.4.p2
  15.7 0.3 collective-permute-start.2
  16.0 3.6 %collective-permute-done.5.p3 = bf16[2,2,128,256]{3,2,1,0:T(8,128)(2,1)S(1)} collective-permute-done((bf16[2,2,128,256]{3,2,1,0:T(8,128)(2,1)}, bf16[2,2,128,256]{3,2,1,0:T(8,128)(2,1)S(1)}, u32[]{:S(2)}, u32[]{:S(2)}) %collective-permute-start.5) | collective-permute-done | bytes 262176 | tf_op jit(solution)/shard_map/ppermute | solution.py:300
  19.6 0.0 collective-permute-done.3.p1
  19.6 0.0 copy-done.2
  19.6 0.0 copy-done.1
  19.6 0.0 copy-start
  19.7 9.3 %shard_map.57.refs_0_ = f32[1024,128]{1,0:T(8,128)S(1)} custom-call(s32[1]{0:T(128)} %bitcast.where_ref, s32[512]{0:T(512)S(1)} %get-tuple-element.32.pairs_ref, s32[512]{0:T(512)S(1)} %get-tuple-element.31.places_ref, s32[16]{0:T(128)S(1)} %pad_add_fusion.spans_ref, bf16[2,2,128,256]{3,2,1,0:T(8,128)(2,1)S(1)} %copy-done.1, ...), custom_call_target="tpu_custom_call" | custom-call | flops 5120000000 | bytes 2097152 | tf_op jit(solution)/shard_map/pallas_call | solution.py:209
  28.9 0.0 collective-permute-done.p1
  28.9 0.9 %collective-permute-done.1.p2 = bf16[2,2,128,256]{3,2,1,0:T(8,128)(2,1)S(1)} collective-permute-done((bf16[2,2,128,256]{3,2,1,0:T(8,128)(2,1)}, bf16[2,2,128,256]{3,2,1,0:T(8,128)(2,1)S(1)}, u32[]{:S(2)}, u32[]{:S(2)}) %collective-permute-start.1) | collective-permute-done | bytes 262176 | tf_op jit(solution)/shard_map/ppermute | solution.py:300
  29.9 0.5 collective-permute-done.2.p3
  30.4 0.0 copy-done
  30.4 9.5 %shard_map.58 = f32[1152,128]{1,0:T(8,128)S(1)} custom-call(s32[1]{0:T(128)} %bitcast.where_ref, s32[512]{0:T(512)S(1)} %get-tuple-element.32.pairs_ref, s32[512]{0:T(512)S(1)} %get-tuple-element.31.places_ref, s32[16]{0:T(128)S(1)} %pad_add_fusion.spans_ref, bf16[2,2,128,256]{3,2,1,0:T(8,128)(2,1)S(1)} %copy-done, ...), custom_call_target="tpu_custom_call" | custom-call | flops 5120000000 | bytes 2097152 | tf_op jit(solution)/shard_map/pallas_call | solution.py:209
  39.9 25.3 %all_to_all.5 = f32[128,1,1152]{2,1,0:T(1,128)S(1)} all-to-all(f32[128,1,1152]{2,1,0:T(1,128)S(1)} %bitcast.9), channel_id=1, replica_groups=mesh['real'=4,'cell'=32] {'real','cell'}, dimensions={0} | all-to-all | bytes 1179648 | tf_op jit(solution)/shard_map/all_to_all | solution.py:308
  65.2 0.9 %shard_map.59 = f32[2,8,2,32]{3,2,1,0:T(2,128)} custom-call(f32[1152,128]{1,0:T(8,128)S(1)} %bitcast.8), custom_call_target="tpu_custom_call" | custom-call | tf_op jit(solution)/shard_map/pallas_call | solution.py:250
  (6 shorter events, 0.1 us)
Async XLA Ops:
  0.0 14.3 %copy-start.4 = (s32[32]{0:T(128)S(1)}, s32[32]{0:T(128)}, u32[]{:S(2)}) copy-start(s32[32]{0:T(128)} %param.8) | copy-start | bytes 388
  0.0 14.5 %copy-start.3 = (s32[512,2]{0,1:T(2,128)S(1)}, s32[512,2]{0,1:T(2,128)}, u32[]{:S(2)}) copy-start(s32[512,2]{0,1:T(2,128)} %param.7) | copy-start | bytes 12292
  0.0 19.6 %copy-start.2 = (s32[2048]{0:T(1024)S(1)}, s32[2048]{0:T(1024)}, u32[]{:S(2)}) copy-start(s32[2048]{0:T(1024)} %param.6) | copy-start | bytes 24580
  3.2 16.4 %copy-start.1 = (bf16[2,2,128,256]{3,2,1,0:T(8,128)(2,1)S(1)}, bf16[2,2,128,256]{3,2,1,0:T(8,128)(2,1)}, u32[]{:S(2)}) copy-start(bf16[2,2,128,256]{3,2,1,0:T(8,128)(2,1)} %get-tuple-element.18.p0) | copy-start | bytes 786436
  3.2 12.5 %collective-permute-start.4 = (bf16[2,2,128,256]{3,2,1,0:T(8,128)(2,1)}, bf16[2,2,128,256]{3,2,1,0:T(8,128)(2,1)S(1)}, u32[]{:S(2)}, u32[]{:S(2)}) collective-permute-start(bf16[2,2,128,256]{3,2,1,0:T(8,128)(2,1)} %get-tuple-element.19), channel_id=1, source_target_pairs={{0,64},{32,96},{64,0},{96,32},{1,65},{33,97},{65,1},{97,33},{2,66}... | collective-permute-start | bytes 786440 | tf_op jit(solution)/shard_map/ppermute | solution.py:300
  7.1 12.6 %collective-permute-start.5 = (bf16[2,2,128,256]{3,2,1,0:T(8,128)(2,1)}, bf16[2,2,128,256]{3,2,1,0:T(8,128)(2,1)S(1)}, u32[]{:S(2)}, u32[]{:S(2)}) collective-permute-start(bf16[2,2,128,256]{3,2,1,0:T(8,128)(2,1)} %get-tuple-element.20), channel_id=1, source_target_pairs={{0,96},{32,0},{64,32},{96,64},{1,97},{33,1},{65,33},{97,65},{2,98}... | collective-permute-start | bytes 786440 | tf_op jit(solution)/shard_map/ppermute | solution.py:300
  7.8 11.8 %collective-permute-start.3 = (bf16[2,2,128,256]{3,2,1,0:T(8,128)(2,1)}, bf16[2,2,128,256]{3,2,1,0:T(8,128)(2,1)S(1)}, u32[]{:S(2)}, u32[]{:S(2)}) collective-permute-start(bf16[2,2,128,256]{3,2,1,0:T(8,128)(2,1)} %get-tuple-element.14.refs_0_), channel_id=1, source_target_pairs={{0,32},{32,64},{64,96},{96,0},{1,33},{33,65},{65,97},{97,1},{2,34}... | collective-permute-start | bytes 786440 | tf_op jit(solution)/shard_map/ppermute | solution.py:300
  11.1 17.9 %collective-permute-start = (bf16[2,2,128,256]{3,2,1,0:T(8,128)(2,1)}, bf16[2,2,128,256]{3,2,1,0:T(8,128)(2,1)S(1)}, u32[]{:S(2)}, u32[]{:S(2)}) collective-permute-start(bf16[2,2,128,256]{3,2,1,0:T(8,128)(2,1)} %get-tuple-element.15), channel_id=1, source_target_pairs={{0,32},{32,64},{64,96},{96,0},{1,33},{33,65},{65,97},{97,1},{2,34}... | collective-permute-start | bytes 786440 | tf_op jit(solution)/shard_map/ppermute | solution.py:300
  11.5 18.3 %collective-permute-start.1 = (bf16[2,2,128,256]{3,2,1,0:T(8,128)(2,1)}, bf16[2,2,128,256]{3,2,1,0:T(8,128)(2,1)S(1)}, u32[]{:S(2)}, u32[]{:S(2)}) collective-permute-start(bf16[2,2,128,256]{3,2,1,0:T(8,128)(2,1)} %get-tuple-element.16), channel_id=1, source_target_pairs={{0,64},{32,96},{64,0},{96,32},{1,65},{33,97},{65,1},{97,33},{2,66}... | collective-permute-start | bytes 786440 | tf_op jit(solution)/shard_map/ppermute | solution.py:300
  15.7 14.6 %collective-permute-start.2 = (bf16[2,2,128,256]{3,2,1,0:T(8,128)(2,1)}, bf16[2,2,128,256]{3,2,1,0:T(8,128)(2,1)S(1)}, u32[]{:S(2)}, u32[]{:S(2)}) collective-permute-start(bf16[2,2,128,256]{3,2,1,0:T(8,128)(2,1)} %get-tuple-element.17), channel_id=1, source_target_pairs={{0,96},{32,0},{64,32},{96,64},{1,97},{33,1},{65,33},{97,65},{2,98}... | collective-permute-start | bytes 786440 | tf_op jit(solution)/shard_map/ppermute | solution.py:300
  19.6 10.7 %copy-start = (bf16[2,2,128,256]{3,2,1,0:T(8,128)(2,1)S(1)}, bf16[2,2,128,256]{3,2,1,0:T(8,128)(2,1)}, u32[]{:S(2)}) copy-start(bf16[2,2,128,256]{3,2,1,0:T(8,128)(2,1)} %get-tuple-element.13.p0) | copy-start | bytes 786436
